TPU v7x, 32 devices: a whole 2x2x4 slice. The times are simulated.
32 devices in a mesh: wide: 16 (over z, y, x), narrow: 2 (over core).
Axes of the slice: x: 2, y: 2, z: 4, core: 2. Of those that a mesh axis runs over, the one named last changes fastest.
Arguments:
- point_owner: int32 [32768, 1], P(('wide', 'narrow')), may hold values from 0 to 15; in each aligned block of 1024 rows (0 to 1023, 1024 to 2047, ...) at most 128 rows name the same one
- point_cell: int32 [32768], P(('wide', 'narrow')), may hold values from 0 to 8191
- normals: float32 [3, 32768], P(None, ('wide', 'narrow')), may hold values from -6 to 6
- strip_count: int32 [32], P(('wide', 'narrow')), may hold values from 1 to 1024, 28672 in all
- neighbours: int32 [16, 2, 2, 27], P('wide', 'narrow'), may hold values from 0 to 18, as said below
Outputs:
- solution: float32 [16, 2, 2, 4096], P('wide', 'narrow')
- residual: float32 [16, 2, 2, 4096], P('wide', 'narrow')
Inputs may be any that keep to these rules, and one draw needn't show every extreme that they name: `point_owner`: the points of one device name each wide index at most 128 times, and some wide index exactly 128 times. `strip_count`: some device has exactly 1024 live points. `neighbours`: entries follow the encoding of the steps; dw and dn are -1, 0 or 1; the relation is mutual (b sees c in a direction exactly when c sees b in the opposite one); entry 13 names the brick itself.
All inputs are finite; a program needn't handle non-finite values.
Results may differ from a plain program's by a relative error of at most 0.0003.
Values sent between devices are 32-bit elements; how exact they have to be, the bound alone decides.
A program may use at most 64 MiB of HBM per device.

v0:
```python
import functools

import jax
import jax.numpy as jnp
from jax import lax
from jax.experimental import pallas as pl
from jax.experimental.pallas import tpu as pltpu
from jax.sharding import PartitionSpec as P

MESH = pl.DeviceIdType.MESH
NT = (((1,), (1,)), ((), ()))
F32 = jnp.float32
BF16 = jnp.bfloat16


def split3(values):
    high = values.astype(BF16).astype(F32)
    rest = values - high
    middle = rest.astype(BF16).astype(F32)
    return high, middle, rest - middle


def one_if(condition):
    return jnp.where(condition, 1.0, 0.0)


def edge(offset):
    return one_if(offset == 0) + 0.5 * one_if((offset == 1) | (offset == -1))


def pack_matrix():
    cell = lax.broadcasted_iota(jnp.int32, (256, 128), 0)
    lane = lax.broadcasted_iota(jnp.int32, (256, 128), 1)
    side, k = (lane // 16) % 4, lane % 16
    wanted = jnp.where(side < 2, k + 240 * side, 16 * k + 15 * (side - 2))
    return one_if(cell == wanted).astype(BF16)


def halo_matrices():
    lane = lax.broadcasted_iota(jnp.int32, (128, 256), 0)
    cell = lax.broadcasted_iota(jnp.int32, (128, 256), 1)
    y, z = cell // 16, cell % 16
    side, k = lane // 16, lane % 16
    face_y = (one_if(side == 0) * one_if(y == 15), one_if(side == 1) * one_if(y == 0))
    face_z = (one_if(side == 2) * one_if(z == 15), one_if(side == 3) * one_if(z == 0))
    corner = (
        one_if((lane == 64) & (y == 15) & (z == 15))
        + one_if((lane == 79) & (y == 15) & (z == 0))
        + one_if((lane == 80) & (y == 0) & (z == 15))
        + one_if((lane == 95) & (y == 0) & (z == 0))
    )
    weight = 0.5 * ((face_y[0] + face_y[1]) * edge(z - k) + (face_z[0] + face_z[1]) * edge(y - k)) + 0.25 * corner
    slope = (face_y[0] - face_y[1]) * one_if(z == k) + (face_z[0] - face_z[1]) * one_if(y == k)
    return weight.astype(BF16), slope.astype(BF16)


def exact_dot(values, matrix):
    rows = values.shape[0]
    parts = jnp.concatenate(split3(values), 0).astype(BF16)
    summed = jnp.dot(parts, matrix, preferred_element_type=F32)
    return summed[:rows] + summed[rows : 2 * rows] + summed[2 * rows :]


def kernel(
    wides, narrows, owner_hbm, cell_hbm, normal_hbm, count_ref, near_ref, solution_ref, residual_ref,
    owner_ref, cell_ref, normal_ref, pack_ref, weight_ref, slope_ref,
    point_out, point_in, vector_src, field_0, field_1, field_2, part_out, part_in,
    in_sem, point_send, point_recv, halo_send, halo_recv, part_send, part_recv,
):
    devices = wides * narrows
    wide = lax.axis_index("wide")
    narrow = lax.axis_index("narrow")
    me = wide * narrows + narrow
    points = cell_ref.shape[1]
    slots = point_out.shape[2]
    loads = [
        pltpu.make_async_copy(source, target, in_sem.at[k])
        for k, (source, target) in enumerate(
            ((owner_hbm, owner_ref), (cell_hbm, cell_ref), (normal_hbm, normal_ref))
        )
    ]
    for load in loads:
        load.start()
    barrier = pltpu.get_barrier_semaphore()

    def after(at, step, count):
        return jnp.where(at + step >= count, at + step - count, at + step)

    def each_device(act):
        if devices > 64:

            @pl.loop(1, devices)
            def _(k):
                other = lax.rem(me + k, devices)
                act((other // narrows, lax.rem(other, narrows)))

            return
        for step in range(1, devices):
            act((wide_after[step // narrows], narrow_after[step % narrows]))

    wide_after = [wide] + [after(wide, k, wides) for k in range(1, wides)]
    narrow_after = [narrow] + [after(narrow, k, narrows) for k in range(1, narrows)]
    each_device(lambda to: pl.semaphore_signal(barrier, inc=1, device_id=to, device_id_type=MESH))

    offsets = [(a, b) for a in (-1, 0, 1) for b in (-1, 0, 1) if (a, b) != (0, 0)]

    def inside(a, b):
        return (wide + a >= 0) & (wide + a < wides) & (narrow + b >= 0) & (narrow + b < narrows)

    sources = (vector_src, field_0, field_1, field_2)
    for source in sources:
        source[18] = jnp.zeros((12, 128), F32)
    for a, b in offsets:
        place = (a + 1) * 3 + b + 1

        @pl.when(jnp.logical_not(inside(a, b)))
        def _(place=place):
            for source in sources:
                source[2 * place : 2 * place + 2] = jnp.zeros((2, 12, 128), F32)

    for load in loads:
        load.wait()

    owner = owner_ref[...]
    live = lax.broadcasted_iota(jnp.int32, (1, points), 1) < count_ref[0]
    owned = lax.broadcasted_iota(jnp.int32, (wides, points), 0) == owner
    owner_hot = one_if(owned)
    blocks = points // 128
    stacked = jnp.concatenate([owner_hot[:, k * 128 : (k + 1) * 128] for k in range(blocks)], 0)
    earlier = jnp.where(
        lax.broadcasted_iota(jnp.int32, (128, 256), 0) < lax.broadcasted_iota(jnp.int32, (128, 256), 1),
        1.0,
        0.0,
    )
    counted = jnp.dot(stacked.astype(BF16), earlier.astype(BF16), preferred_element_type=F32)
    ranks = []
    before = jnp.zeros((wides, 128), F32)
    for k in range(blocks):
        rows = slice(k * wides, (k + 1) * wides)
        ranks.append(
            jnp.sum(stacked[rows] * (counted[rows, :128] + before), axis=0, keepdims=True)
        )
        before = before + counted[rows, 128:]
    rank = jnp.concatenate(ranks, 1).astype(jnp.int32)
    code = jnp.where(live, cell_ref[...] + 1, 0)
    rows = [lax.shift_right_logical(code, 8).astype(F32), (code & 255).astype(F32)]
    for c in range(3):
        rows.extend(split3(normal_ref[c : c + 1]))
    weighted = jnp.concatenate([jnp.where(owned, row, 0.0) for row in rows], 0).astype(BF16)
    rank_hot = one_if(lax.broadcasted_iota(jnp.int32, (slots, points), 0) == rank).astype(BF16)
    moved = lax.dot_general(weighted, rank_hot, NT, preferred_element_type=F32)
    moved = [moved[k * wides : (k + 1) * wides] for k in range(11)]
    values = [moved[2 + 3 * c] + moved[3 + 3 * c] + moved[4 + 3 * c] for c in range(3)]
    values.append(256.0 * moved[0] + moved[1])
    for k in range(wides):
        for c in range(4):
            point_out[k, c : c + 1] = values[c][k : k + 1]

    pl.semaphore_wait(barrier, devices - 1)

    for other in wide_after[1:]:
        pltpu.make_async_remote_copy(
            src_ref=point_out.at[other],
            dst_ref=point_in.at[wide],
            send_sem=point_send.at[0],
            recv_sem=point_recv.at[0],
            device_id=(other, narrow),
            device_id_type=MESH,
        ).start()

    pack_ref[...] = pack_matrix()
    weight_ref[...], slope_ref[...] = halo_matrices()
    point_in[pl.ds(wide, 1)] = point_out[pl.ds(wide, 1)]
    arrived = point_in.at[pl.ds(0, wides - 1)]
    pltpu.make_async_copy(arrived, arrived, point_recv.at[0]).wait()

    group = 8 if slots % 128 == 0 and wides % 8 == 0 else 1
    splatted = jnp.zeros((320, 256), F32)
    for k in range(0, wides, group):
        got = jnp.concatenate([point_in[k + j] for j in range(group)], 1)
        width = group * slots
        cell = got[3:4].astype(jnp.int32) - 1
        row_hot = lax.broadcasted_iota(jnp.int32, (32, width), 0) == lax.shift_right_arithmetic(cell, 8)
        lane_hot = lax.broadcasted_iota(jnp.int32, (256, width), 0) == (cell & 255)
        weights = []
        for c in range(3):
            weights.extend(split3(got[c : c + 1]))
        weights.append(jnp.ones((1, width), F32))
        weighted = jnp.concatenate([jnp.where(row_hot, w, 0.0) for w in weights], 0).astype(BF16)
        splatted = splatted + lax.dot_general(
            weighted, jnp.where(lane_hot, 1.0, 0.0).astype(BF16), NT, preferred_element_type=F32
        )
    vectors = [
        splatted[96 * c : 96 * c + 32] + splatted[96 * c + 32 : 96 * c + 64] + splatted[96 * c + 64 : 96 * c + 96]
        for c in range(3)
    ]
    shifted_diagonal = 16.5 + 2.0 * splatted[288:320]

    def halo(source, turn, begin):
        for a, b in offsets:
            place = (a + 1) * 3 + b + 1

            @pl.when(inside(a, b))
            def _(a=a, b=b, place=place):
                if begin:
                    pltpu.make_async_remote_copy(
                        src_ref=source.at[pl.ds(8, 2)],
                        dst_ref=source.at[pl.ds(2 * (8 - place), 2)],
                        send_sem=halo_send.at[turn, place],
                        recv_sem=halo_recv.at[turn, 8 - place],
                        device_id=(wide + a, narrow + b),
                        device_id_type=MESH,
                    ).start()
                else:
                    got = source.at[pl.ds(2 * place, 2)]
                    pltpu.make_async_copy(got, got, halo_recv.at[turn, place]).wait()

    def near(brick, a, b, c):
        return near_ref[0, 0, brick, (a + 1) * 9 + (b + 1) * 3 + c + 1]

    cell_at = lax.broadcasted_iota(jnp.int32, (32, 256), 1)
    x_at = lax.broadcasted_iota(jnp.int32, (32, 256), 0) % 16
    y_at, z_at = cell_at // 16, cell_at % 16
    low_half = lax.broadcasted_iota(jnp.int32, (8, 128), 1) < 64

    def send_faces(turn, ends, packed):
        source = sources[turn]
        for brick in range(2):
            row = 16 * brick
            source[8 + brick, 0:8] = jnp.where(low_half, packed[row : row + 8], packed[row + 8 : row + 16])
            for k, x in enumerate((0, 15)):
                for half in range(2):
                    at = 8 + 2 * k + half
                    source[8 + brick, at : at + 1] = ends[row + x : row + x + 1, 128 * half : 128 * half + 128]
        halo(source, turn, True)

    def ends_of(source):
        rows = []
        for brick in range(2):
            low, high = near(brick, -1, 0, 0), near(brick, 1, 0, 0)
            low = jnp.concatenate([source[low, 10:11, :], source[low, 11:12, :]], 1)
            high = jnp.concatenate([source[high, 8:9, :], source[high, 9:10, :]], 1)
            rows.append((low, high))
        low = jnp.concatenate([jnp.broadcast_to(rows[brick][0], (16, 256)) for brick in range(2)], 0)
        high = jnp.concatenate([jnp.broadcast_to(rows[brick][1], (16, 256)) for brick in range(2)], 0)
        return low, high

    def merged(source, brick, a, rows, corners):
        lane = lax.broadcasted_iota(jnp.int32, (rows.stop - rows.start, 128), 1) % 64

        def beside(b, c):
            return source[near(brick, a, b, c), rows, :]

        faces = jnp.where(
            lane < 32,
            jnp.where(lane < 16, beside(1, 0), beside(-1, 0)),
            jnp.where(lane < 48, beside(0, 1), beside(0, -1)),
        )
        if not corners:
            return faces, faces
        corner = jnp.where(
            lane < 16,
            jnp.where(lane == 0, beside(1, 1), beside(1, -1)),
            jnp.where(lane == 16, beside(-1, 1), beside(-1, -1)),
        )
        return faces, corner

    def swap(values):
        return pltpu.roll(values, 64, 1)

    def faces_of(source, brick, corners):
        faces, corner = merged(source, brick, 0, slice(0, 8), corners)
        return jnp.concatenate(
            [jnp.where(low_half, faces, swap(corner)), jnp.where(low_half, swap(faces), corner)], 0
        )

    send_faces(
        0,
        vectors[0],
        jnp.where(
            lax.broadcasted_iota(jnp.int32, (32, 128), 1) % 64 < 32,
            exact_dot(vectors[1], pack_ref[...]),
            exact_dot(vectors[2], pack_ref[...]),
        ),
    )
    change = (
        jnp.where(x_at == 15, 0.0, pltpu.roll(vectors[0], 31, 0))
        - jnp.where(x_at == 0, 0.0, pltpu.roll(vectors[0], 1, 0))
        + jnp.where(y_at == 15, 0.0, pltpu.roll(vectors[1], 240, 1))
        - jnp.where(y_at == 0, 0.0, pltpu.roll(vectors[1], 16, 1))
        + jnp.where(z_at == 15, 0.0, pltpu.roll(vectors[2], 255, 1))
        - jnp.where(z_at == 0, 0.0, pltpu.roll(vectors[2], 1, 1))
    )
    halo(vector_src, 0, False)
    low, high = ends_of(vector_src)
    faces = jnp.concatenate([faces_of(vector_src, brick, False) for brick in range(2)], 0)
    change = (
        change
        + jnp.where(x_at == 15, high, 0.0)
        - jnp.where(x_at == 0, low, 0.0)
        + exact_dot(faces, slope_ref[...])
    )
    residual = -4.0 * change

    def pack(values):
        return exact_dot(values, pack_ref[...])

    def plane_sum(values):
        summed = values + 0.5 * (
            jnp.where(z_at == 0, 0.0, pltpu.roll(values, 1, 1))
            + jnp.where(z_at == 15, 0.0, pltpu.roll(values, 255, 1))
        )
        return summed + 0.5 * (
            jnp.where(y_at == 0, 0.0, pltpu.roll(summed, 16, 1))
            + jnp.where(y_at == 15, 0.0, pltpu.roll(summed, 240, 1))
        )

    def operator(turn, values):
        source = sources[1 + turn]
        inner = values + 0.5 * (
            jnp.where(x_at == 0, 0.0, pltpu.roll(values, 1, 0))
            + jnp.where(x_at == 15, 0.0, pltpu.roll(values, 31, 0))
        )
        own = shifted_diagonal * values - 2.0 * plane_sum(inner)
        halo(source, 1 + turn, False)
        low, high = ends_of(source)
        ends = plane_sum(jnp.where(x_at == 0, low, jnp.where(x_at == 15, high, 0.0)))
        row_at = lax.broadcasted_iota(jnp.int32, (16, 128), 0)
        half_row = lax.broadcasted_iota(jnp.int32, (1, 128), 1) < 64
        faces = []
        for brick in range(2):
            here = faces_of(source, brick, True)
            face, corner = merged(source, brick, -1, slice(7, 8), True)
            low = jnp.where(half_row, swap(face), corner)
            face, corner = merged(source, brick, 1, slice(0, 1), True)
            high = jnp.where(half_row, face, swap(corner))
            faces.append(
                here
                + 0.5
                * (
                    jnp.where(row_at == 0, low, pltpu.roll(here, 1, 0))
                    + jnp.where(row_at == 15, high, pltpu.roll(here, 15, 0))
                )
            )
        return own - ends - 2.0 * exact_dot(jnp.concatenate(faces, 0), weight_ref[...])

    def send_sums(turn, one, two):
        for row, values in enumerate((one, two)):
            summed = jnp.sum(values, axis=0, keepdims=True)
            part_out[turn, row : row + 1] = summed[:, :128] + summed[:, 128:]
        part_in[turn, pl.ds(me, 1)] = part_out[pl.ds(turn, 1)]

        each_device(
            lambda to: pltpu.make_async_remote_copy(
                src_ref=part_out.at[turn],
                dst_ref=part_in.at[turn, me],
                send_sem=part_send.at[turn],
                recv_sem=part_recv.at[turn],
                device_id=to,
                device_id_type=MESH,
            ).start()
        )

    def get_sums(turn):
        got = part_in.at[turn, pl.ds(0, devices - 1)]
        pltpu.make_async_copy(got, got, part_recv.at[turn]).wait()
        total = jnp.sum(jnp.sum(part_in[turn], axis=0), axis=1, keepdims=True)
        return total[0:1], total[1:2]

    send_faces(1, residual, pack(residual))
    image = operator(0, residual)

    packed = pack(image)
    send_faces(2, image, packed)
    send_sums(0, residual * residual, residual * image)
    second = operator(1, image)
    packed_second = pack(second)
    square_0, product = get_sums(0)
    step_0 = square_0 / product
    answer = step_0 * residual
    towards, towards_image, towards_second = residual, image, second
    residual = residual - step_0 * image
    image = image - step_0 * second
    packed = packed - step_0 * packed_second

    send_faces(3, image, packed)
    send_sums(1, residual * residual, residual * image)
    second = operator(2, image)
    square_1, product = get_sums(1)
    ratio = square_1 / square_0
    step_1 = square_1 / (product - ratio * square_1 / step_0)
    towards = residual + ratio * towards
    towards_image = image + ratio * towards_image
    towards_second = second + ratio * towards_second
    answer = answer + step_1 * towards
    residual = residual - step_1 * towards_image
    image = image - step_1 * towards_second

    send_sums(2, residual * residual, residual * image)
    square_2, product = get_sums(2)
    ratio = square_2 / square_1
    step_2 = square_2 / (product - ratio * square_2 / step_1)
    towards = residual + ratio * towards
    towards_image = image + ratio * towards_image
    answer = answer + step_2 * towards
    residual = residual - step_2 * towards_image

    for brick in range(2):
        for x in range(16):
            at = (0, 0, slice(brick, brick + 1), slice(256 * x, 256 * x + 256))
            solution_ref[at] = answer[16 * brick + x : 16 * brick + x + 1]
            residual_ref[at] = residual[16 * brick + x : 16 * brick + x + 1]

    sent = point_out.at[pl.ds(0, wides - 1)]
    pltpu.make_async_copy(sent, sent, point_send.at[0]).wait()
    for turn in range(3):
        sent = part_in.at[turn, pl.ds(0, devices - 1)]
        pltpu.make_async_copy(sent, sent, part_send.at[turn]).wait()
    for a, b in offsets:
        place = (a + 1) * 3 + b + 1

        @pl.when(inside(a, b))
        def _(place=place):
            for turn, source in enumerate(sources):
                sent = source.at[pl.ds(8, 2)]
                pltpu.make_async_copy(sent, sent, halo_send.at[turn, place]).wait()


def shards(wides, narrows, point_owner, point_cell, normals, strip_count, neighbours):
    points = point_cell.shape[0]
    devices = wides * narrows
    slots = 2 * points // wides
    vmem = pl.BlockSpec(memory_space=pltpu.VMEM)
    hbm = pl.BlockSpec(memory_space=pltpu.HBM)
    smem = pl.BlockSpec(memory_space=pltpu.SMEM)
    out = jax.ShapeDtypeStruct((1, 1, 2, 4096), F32)
    return pl.pallas_call(
        functools.partial(kernel, wides, narrows),
        out_shape=(out, out),
        in_specs=[hbm, hbm, hbm, smem, smem],
        out_specs=(vmem, vmem),
        scratch_shapes=[
            pltpu.VMEM((1, points), jnp.int32),
            pltpu.VMEM((1, points), jnp.int32),
            pltpu.VMEM((3, points), F32),
            pltpu.VMEM((256, 128), BF16),
            pltpu.VMEM((128, 256), BF16),
            pltpu.VMEM((128, 256), BF16),
            pltpu.VMEM((wides, 4, slots), F32),
            pltpu.VMEM((wides, 4, slots), F32),
            pltpu.VMEM((19, 12, 128), F32),
            pltpu.VMEM((19, 12, 128), F32),
            pltpu.VMEM((19, 12, 128), F32),
            pltpu.VMEM((19, 12, 128), F32),
            pltpu.VMEM((3, 2, 128), F32),
            pltpu.VMEM((3, devices, 2, 128), F32),
            pltpu.SemaphoreType.DMA((3,)),
            pltpu.SemaphoreType.DMA((1,)),
            pltpu.SemaphoreType.DMA((1,)),
            pltpu.SemaphoreType.DMA((4, 9)),
            pltpu.SemaphoreType.DMA((4, 9)),
            pltpu.SemaphoreType.DMA((3,)),
            pltpu.SemaphoreType.DMA((3,)),
        ],
        compiler_params=pltpu.CompilerParams(
            collective_id=0, has_side_effects=True, vmem_limit_bytes=32 * 1024 * 1024
        ),
    )(
        point_owner.reshape(1, points), point_cell.reshape(1, points), normals, strip_count, neighbours
    )


def solution(mesh):
    return jax.shard_map(
        functools.partial(shards, mesh.shape["wide"], mesh.shape["narrow"]),
        mesh=mesh,
        in_specs=(
            P(("wide", "narrow"), None),
            P(("wide", "narrow")),
            P(None, ("wide", "narrow")),
            P(("wide", "narrow")),
            P("wide", "narrow", None, None),
        ),
        out_specs=(P("wide", "narrow", None, None), P("wide", "narrow", None, None)),
        check_vma=False,
    )
```

profile of v0, /device:TPU:0, one launch (start us, length us, event | category | flops | bytes accessed | tf_op | source)
XLA Modules:
  0.0 39.5 jit_solution(15946112134878139102)
XLA Ops:
  0.6 0.0 copy-start.1
  1.3 0.0 copy-start.3
  1.3 0.0 copy-done.1
  1.3 0.7 %copy-done.3 = s32[1,1,2,27]{3,2,1,0:T(2,128)S(1)} copy-done((s32[1,1,2,27]{3,2,1,0:T(2,128)S(1)}, s32[1,1,2,27]{3,2,1,0:T(2,128)}, u32[]{:S(2)}) %copy-start.3) | copy-done | bytes 240
  2.0 0.0 copy-start
  2.0 0.7 %copy-done = f32[3,1024]{1,0:T(4,128)S(1)} copy-done((f32[3,1024]{1,0:T(4,128)S(1)}, f32[3,1024]{1,0:T(4,128)}, u32[]{:S(2)}) %copy-start) | copy-done | bytes 12312
  2.7 0.0 copy-start.2
  2.7 0.7 %copy-done.2 = s32[1024]{0:T(1024)S(1)} copy-done((s32[1024]{0:T(1024)S(1)}, s32[1024]{0:T(1024)}, u32[]{:S(2)}) %copy-start.2) | copy-done | bytes 4120
  3.4 34.9 %shard_map.68 = (f32[1,1,2,4096]{3,2,1,0:T(2,128)S(1)}, f32[1,1,2,4096]{3,2,1,0:T(2,128)S(1)}) custom-call(s32[1,1024]{1,0:T(1,128)S(1)} %bitcast.2, s32[1,1024]{1,0:T(1,128)S(1)} %bitcast.3, f32[3,1024]{1,0:T(4,128)S(1)} %copy-done, s32[1]{0:T(128)S(6)} %copy.9.count_ref, s32[1,1,2,27]{3,2,1,0:T(2,128)S(1)} %copy-done.3), custom_call_target="tpu_custom_call" | custom-call | tf_op jit(solution)/shard_map/pallas_call | solution.py:437
  38.3 0.6 %copy.10 = f32[1,1,2,4096]{3,2,1,0:T(2,128)} copy(f32[1,1,2,4096]{3,2,1,0:T(2,128)S(1)} %get-tuple-element.4) | data formatting | bytes 65536
  38.9 0.6 %copy.11 = f32[1,1,2,4096]{3,2,1,0:T(2,128)} copy(f32[1,1,2,4096]{3,2,1,0:T(2,128)S(1)} %get-tuple-element.5) | data formatting | bytes 65536
Async XLA Ops:
  0.6 0.7 %copy-start.1 = (s32[1024,1]{0,1:T(1,128)S(1)}, s32[1024,1]{0,1:T(1,128)}, u32[]{:S(2)}) copy-start(s32[1024,1]{0,1:T(1,128)} %param.5) | copy-start | bytes 12292
  1.3 0.7 %copy-start.3 = (s32[1,1,2,27]{3,2,1,0:T(2,128)S(1)}, s32[1,1,2,27]{3,2,1,0:T(2,128)}, u32[]{:S(2)}) copy-start(s32[1,1,2,27]{3,2,1,0:T(2,128)} %near_ref.1) | copy-start | bytes 652
  2.0 0.7 %copy-start = (f32[3,1024]{1,0:T(4,128)S(1)}, f32[3,1024]{1,0:T(4,128)}, u32[]{:S(2)}) copy-start(f32[3,1024]{1,0:T(4,128)} %normal_hbm.1) | copy-start | bytes 36868
  2.7 0.7 %copy-start.2 = (s32[1024]{0:T(1024)S(1)}, s32[1024]{0:T(1024)}, u32[]{:S(2)}) copy-start(s32[1024]{0:T(1024)} %param.6) | copy-start | bytes 12292
where the time goes:
time: 39.8 us; the launch traced here: 39.5 us
  Pallas kernels  34.9 us (88%)
  local copies, waits for them, and re-layouts  3.31 us (8%)
  between operations  1.32 us (3%)
    pallas_call x1, Pallas kernels, shards(): pl.pallas_call(functools.partial(kernel, wides, narrows), out_shape=(out,...  34.9 us
    unnamed x10, local copies, waits for them, and re-layouts  3.31 us

commit v1 on v0

--- a/solution.py
+++ b/solution.py
@@ -95,14 +95,26 @@
                 act((other // narrows, lax.rem(other, narrows)))
 
             return
-        for step in range(1, devices):
-            act((wide_after[step // narrows], narrow_after[step % narrows]))
-
-    wide_after = [wide] + [after(wide, k, wides) for k in range(1, wides)]
+        for to_wide in far_first + [wide]:
+            for to_narrow in narrow_after[::-1]:
+                if to_wide is not wide or to_narrow is not narrow:
+                    act((to_wide, to_narrow))
+
+    far_first = []
+    if wides & (wides - 1):
+        far_first = [after(wide, k, wides) for k in range(1, wides)]
+    else:
+        flips = []
+        bit = 1
+        while bit < wides:
+            flips.append((1 - 2 * (lax.div(wide, bit) % 2)) * bit)
+            bit = 2 * bit
+        for k in range(wides - 1, 0, -1):
+            far_first.append(wide + sum(flip for j, flip in enumerate(flips) if k >> j & 1))
     narrow_after = [narrow] + [after(narrow, k, narrows) for k in range(1, narrows)]
     each_device(lambda to: pl.semaphore_signal(barrier, inc=1, device_id=to, device_id_type=MESH))
 
-    offsets = [(a, b) for a in (-1, 0, 1) for b in (-1, 0, 1) if (a, b) != (0, 0)]
+    offsets = [(a, b) for a in (1, -1, 0) for b in (-1, 1, 0) if (a, b) != (0, 0)]
 
     def inside(a, b):
         return (wide + a >= 0) & (wide + a < wides) & (narrow + b >= 0) & (narrow + b < narrows)
@@ -158,7 +170,7 @@
 
     pl.semaphore_wait(barrier, devices - 1)
 
-    for other in wide_after[1:]:
+    for other in far_first:
         pltpu.make_async_remote_copy(
             src_ref=point_out.at[other],
             dst_ref=point_in.at[wide],
@@ -344,12 +356,11 @@
             )
         return own - ends - 2.0 * exact_dot(jnp.concatenate(faces, 0), weight_ref[...])
 
-    def send_sums(turn, one, two):
-        for row, values in enumerate((one, two)):
+    def send_sums(turn, products):
+        for row, values in enumerate(products):
             summed = jnp.sum(values, axis=0, keepdims=True)
             part_out[turn, row : row + 1] = summed[:, :128] + summed[:, 128:]
         part_in[turn, pl.ds(me, 1)] = part_out[pl.ds(turn, 1)]
-
         each_device(
             lambda to: pltpu.make_async_remote_copy(
                 src_ref=part_out.at[turn],
@@ -365,30 +376,28 @@
         got = part_in.at[turn, pl.ds(0, devices - 1)]
         pltpu.make_async_copy(got, got, part_recv.at[turn]).wait()
         total = jnp.sum(jnp.sum(part_in[turn], axis=0), axis=1, keepdims=True)
-        return total[0:1], total[1:2]
+        return total[0:1], total[1:2], total[2:3], total[3:4]
 
     send_faces(1, residual, pack(residual))
     image = operator(0, residual)
 
-    packed = pack(image)
-    send_faces(2, image, packed)
-    send_sums(0, residual * residual, residual * image)
+    send_faces(2, image, pack(image))
     second = operator(1, image)
-    packed_second = pack(second)
-    square_0, product = get_sums(0)
+
+    send_faces(3, second, pack(second))
+    send_sums(0, (residual * residual, residual * image, image * image, image * second))
+    third = operator(2, second)
+    square_0, product, square_image, product_image = get_sums(0)
     step_0 = square_0 / product
+    square_1 = step_0 * step_0 * square_image - square_0
+    product = product - 2.0 * step_0 * square_image + step_0 * step_0 * product_image
+    ratio = square_1 / square_0
+    step_1 = square_1 / (product - ratio * square_1 / step_0)
     answer = step_0 * residual
     towards, towards_image, towards_second = residual, image, second
     residual = residual - step_0 * image
     image = image - step_0 * second
-    packed = packed - step_0 * packed_second
-
-    send_faces(3, image, packed)
-    send_sums(1, residual * residual, residual * image)
-    second = operator(2, image)
-    square_1, product = get_sums(1)
-    ratio = square_1 / square_0
-    step_1 = square_1 / (product - ratio * square_1 / step_0)
+    second = second - step_0 * third
     towards = residual + ratio * towards
     towards_image = image + ratio * towards_image
     towards_second = second + ratio * towards_second
@@ -396,8 +405,9 @@
     residual = residual - step_1 * towards_image
     image = image - step_1 * towards_second
 
-    send_sums(2, residual * residual, residual * image)
-    square_2, product = get_sums(2)
+    square, product = residual * residual, residual * image
+    send_sums(1, (square, product, square, product))
+    square_2, product, _, _ = get_sums(1)
     ratio = square_2 / square_1
     step_2 = square_2 / (product - ratio * square_2 / step_1)
     towards = residual + ratio * towards
@@ -413,7 +423,7 @@
 
     sent = point_out.at[pl.ds(0, wides - 1)]
     pltpu.make_async_copy(sent, sent, point_send.at[0]).wait()
-    for turn in range(3):
+    for turn in range(2):
         sent = part_in.at[turn, pl.ds(0, devices - 1)]
         pltpu.make_async_copy(sent, sent, part_send.at[turn]).wait()
     for a, b in offsets:
@@ -452,8 +462,8 @@
             pltpu.VMEM((19, 12, 128), F32),
             pltpu.VMEM((19, 12, 128), F32),
             pltpu.VMEM((19, 12, 128), F32),
-            pltpu.VMEM((3, 2, 128), F32),
-            pltpu.VMEM((3, devices, 2, 128), F32),
+            pltpu.VMEM((2, 4, 128), F32),
+            pltpu.VMEM((2, devices, 4, 128), F32),
             pltpu.SemaphoreType.DMA((3,)),
             pltpu.SemaphoreType.DMA((1,)),
             pltpu.SemaphoreType.DMA((1,)),

time: 39.8 us -> 39.5 us (level)
  no operation moved by 1% of the time
where the time goes in v1:
time: 39.5 us; the launch traced here: 39.2 us
  Pallas kernels  34.6 us (88%)
  local copies, waits for them, and re-layouts  3.31 us (8%)
  between operations  1.32 us (3%)
    pallas_call x1, Pallas kernels, shards(): pl.pallas_call(functools.partial(kernel, wides, narrows), out_shape=(out,...  34.6 us
    unnamed x10, local copies, waits for them, and re-layouts  3.31 us

profile of v1, /device:TPU:0, one launch (start us, length us, event | category | flops | bytes accessed | tf_op | source)
XLA Modules:
  0.0 39.2 jit_solution(15245118105163526766)
XLA Ops:
  0.6 0.0 copy-start.1
  1.3 0.0 copy-start.3
  1.3 0.0 copy-done.1
  1.3 0.7 %copy-done.3 = s32[1,1,2,27]{3,2,1,0:T(2,128)S(1)} copy-done((s32[1,1,2,27]{3,2,1,0:T(2,128)S(1)}, s32[1,1,2,27]{3,2,1,0:T(2,128)}, u32[]{:S(2)}) %copy-start.3) | copy-done | bytes 240
  2.0 0.0 copy-start
  2.0 0.7 %copy-done = f32[3,1024]{1,0:T(4,128)S(1)} copy-done((f32[3,1024]{1,0:T(4,128)S(1)}, f32[3,1024]{1,0:T(4,128)}, u32[]{:S(2)}) %copy-start) | copy-done | bytes 12312
  2.7 0.0 copy-start.2
  2.7 0.7 %copy-done.2 = s32[1024]{0:T(1024)S(1)} copy-done((s32[1024]{0:T(1024)S(1)}, s32[1024]{0:T(1024)}, u32[]{:S(2)}) %copy-start.2) | copy-done | bytes 4120
  3.4 34.6 %shard_map.68 = (f32[1,1,2,4096]{3,2,1,0:T(2,128)S(1)}, f32[1,1,2,4096]{3,2,1,0:T(2,128)S(1)}) custom-call(s32[1,1024]{1,0:T(1,128)S(1)} %bitcast.2, s32[1,1024]{1,0:T(1,128)S(1)} %bitcast.3, f32[3,1024]{1,0:T(4,128)S(1)} %copy-done, s32[1]{0:T(128)S(6)} %copy.9.count_ref, s32[1,1,2,27]{3,2,1,0:T(2,128)S(1)} %copy-done.3), custom_call_target="tpu_custom_call" | custom-call | tf_op jit(solution)/shard_map/pallas_call | solution.py:447
  38.0 0.6 %copy.10 = f32[1,1,2,4096]{3,2,1,0:T(2,128)} copy(f32[1,1,2,4096]{3,2,1,0:T(2,128)S(1)} %get-tuple-element.4) | data formatting | bytes 65536
  38.6 0.6 %copy.11 = f32[1,1,2,4096]{3,2,1,0:T(2,128)} copy(f32[1,1,2,4096]{3,2,1,0:T(2,128)S(1)} %get-tuple-element.5) | data formatting | bytes 65536
Async XLA Ops:
  0.6 0.7 %copy-start.1 = (s32[1024,1]{0,1:T(1,128)S(1)}, s32[1024,1]{0,1:T(1,128)}, u32[]{:S(2)}) copy-start(s32[1024,1]{0,1:T(1,128)} %param.5) | copy-start | bytes 12292
  1.3 0.7 %copy-start.3 = (s32[1,1,2,27]{3,2,1,0:T(2,128)S(1)}, s32[1,1,2,27]{3,2,1,0:T(2,128)}, u32[]{:S(2)}) copy-start(s32[1,1,2,27]{3,2,1,0:T(2,128)} %near_ref.1) | copy-start | bytes 652
  2.0 0.7 %copy-start = (f32[3,1024]{1,0:T(4,128)S(1)}, f32[3,1024]{1,0:T(4,128)}, u32[]{:S(2)}) copy-start(f32[3,1024]{1,0:T(4,128)} %normal_hbm.1) | copy-start | bytes 36868
  2.7 0.7 %copy-start.2 = (s32[1024]{0:T(1024)S(1)}, s32[1024]{0:T(1024)}, u32[]{:S(2)}) copy-start(s32[1024]{0:T(1024)} %param.6) | copy-start | bytes 12292

commit v2 on v0

--- a/solution.py
+++ b/solution.py
@@ -54,6 +54,16 @@
     return weight.astype(BF16), slope.astype(BF16)
 
 
+def plane_matrix():
+    one = lax.broadcasted_iota(jnp.int32, (256, 256), 0)
+    two = lax.broadcasted_iota(jnp.int32, (256, 256), 1)
+    return (edge(one // 16 - two // 16) * edge(one % 16 - two % 16)).astype(BF16)
+
+
+def with_packed(matrix, selection):
+    return jnp.concatenate([matrix, jnp.dot(matrix, selection, preferred_element_type=F32).astype(BF16)], 1)
+
+
 def exact_dot(values, matrix):
     rows = values.shape[0]
     parts = jnp.concatenate(split3(values), 0).astype(BF16)
@@ -63,7 +73,7 @@
 
 def kernel(
     wides, narrows, owner_hbm, cell_hbm, normal_hbm, count_ref, near_ref, solution_ref, residual_ref,
-    owner_ref, cell_ref, normal_ref, pack_ref, weight_ref, slope_ref,
+    owner_ref, cell_ref, normal_ref, pack_ref, weight_ref, slope_ref, plane_ref,
     point_out, point_in, vector_src, field_0, field_1, field_2, part_out, part_in,
     in_sem, point_send, point_recv, halo_send, halo_recv, part_send, part_recv,
 ):
@@ -81,6 +91,12 @@
     ]
     for load in loads:
         load.start()
+    sources = (vector_src, field_0, field_1, field_2)
+    for source in sources:
+        for place in range(19):
+            if place // 2 != 4:
+                source[place] = jnp.zeros((12, 128), F32)
+
     barrier = pltpu.get_barrier_semaphore()
 
     def after(at, step, count):
@@ -95,28 +111,52 @@
                 act((other // narrows, lax.rem(other, narrows)))
 
             return
-        for step in range(1, devices):
-            act((wide_after[step // narrows], narrow_after[step % narrows]))
-
-    wide_after = [wide] + [after(wide, k, wides) for k in range(1, wides)]
+        for to_wide in far_first + [wide]:
+            for to_narrow in narrow_after[::-1]:
+                if to_wide is not wide or to_narrow is not narrow:
+                    act((to_wide, to_narrow))
+
+    far_first = []
+    if wides & (wides - 1):
+        far_first = [after(wide, k, wides) for k in range(1, wides)]
+    else:
+        flips = []
+        bit = 1
+        while bit < wides:
+            flips.append((1 - 2 * (lax.div(wide, bit) % 2)) * bit)
+            bit = 2 * bit
+        for k in range(wides - 1, 0, -1):
+            far_first.append(wide + sum(flip for j, flip in enumerate(flips) if k >> j & 1))
     narrow_after = [narrow] + [after(narrow, k, narrows) for k in range(1, narrows)]
     each_device(lambda to: pl.semaphore_signal(barrier, inc=1, device_id=to, device_id_type=MESH))
 
-    offsets = [(a, b) for a in (-1, 0, 1) for b in (-1, 0, 1) if (a, b) != (0, 0)]
-
-    def inside(a, b):
-        return (wide + a >= 0) & (wide + a < wides) & (narrow + b >= 0) & (narrow + b < narrows)
-
-    sources = (vector_src, field_0, field_1, field_2)
-    for source in sources:
-        source[18] = jnp.zeros((12, 128), F32)
-    for a, b in offsets:
-        place = (a + 1) * 3 + b + 1
-
-        @pl.when(jnp.logical_not(inside(a, b)))
-        def _(place=place):
-            for source in sources:
-                source[2 * place : 2 * place + 2] = jnp.zeros((2, 12, 128), F32)
+    if narrows == 2:
+        turns = (1 - 2 * narrow,)
+    else:
+        turns = (-1, 1)
+    groups = []
+    for a in (1, -1):
+        there = (wide + a >= 0) & (wide + a < wides)
+        if narrows == 2:
+            groups.append((there, [(a, turns[0]), (a, 0)]))
+        else:
+            groups.append((there, [(a, 0)]))
+            for b in turns:
+                groups.append((there & (narrow + b >= 0) & (narrow + b < narrows), [(a, b)]))
+    for b in turns:
+        groups.append((None if narrows == 2 else (narrow + b >= 0) & (narrow + b < narrows), [(0, b)]))
+
+    def each_beside(act):
+        for there, peers in groups:
+
+            def body(peers=peers):
+                for a, b in peers:
+                    act(a, b, (a + 1) * 3 + b + 1)
+
+            if there is None:
+                body()
+            else:
+                pl.when(there)(body)
 
     for load in loads:
         load.wait()
@@ -158,7 +198,7 @@
 
     pl.semaphore_wait(barrier, devices - 1)
 
-    for other in wide_after[1:]:
+    for other in far_first:
         pltpu.make_async_remote_copy(
             src_ref=point_out.at[other],
             dst_ref=point_in.at[wide],
@@ -169,7 +209,10 @@
         ).start()
 
     pack_ref[...] = pack_matrix()
-    weight_ref[...], slope_ref[...] = halo_matrices()
+    weight, slope = halo_matrices()
+    weight_ref[...] = with_packed(weight, pack_ref[...])
+    slope_ref[...] = with_packed(slope, pack_ref[...])
+    plane_ref[...] = with_packed(plane_matrix(), pack_ref[...])
     point_in[pl.ds(wide, 1)] = point_out[pl.ds(wide, 1)]
     arrived = point_in.at[pl.ds(0, wides - 1)]
     pltpu.make_async_copy(arrived, arrived, point_recv.at[0]).wait()
@@ -196,24 +239,25 @@
     ]
     shifted_diagonal = 16.5 + 2.0 * splatted[288:320]
 
-    def halo(source, turn, begin):
-        for a, b in offsets:
-            place = (a + 1) * 3 + b + 1
-
-            @pl.when(inside(a, b))
-            def _(a=a, b=b, place=place):
-                if begin:
-                    pltpu.make_async_remote_copy(
-                        src_ref=source.at[pl.ds(8, 2)],
-                        dst_ref=source.at[pl.ds(2 * (8 - place), 2)],
-                        send_sem=halo_send.at[turn, place],
-                        recv_sem=halo_recv.at[turn, 8 - place],
-                        device_id=(wide + a, narrow + b),
-                        device_id_type=MESH,
-                    ).start()
-                else:
-                    got = source.at[pl.ds(2 * place, 2)]
-                    pltpu.make_async_copy(got, got, halo_recv.at[turn, place]).wait()
+    def halo_start(source, turn):
+        def start(a, b, place):
+            pltpu.make_async_remote_copy(
+                src_ref=source.at[pl.ds(8, 2)],
+                dst_ref=source.at[pl.ds(2 * (8 - place), 2)],
+                send_sem=halo_send.at[turn, place],
+                recv_sem=halo_recv.at[turn, 8 - place],
+                device_id=(wide + a, narrow + b),
+                device_id_type=MESH,
+            ).start()
+
+        each_beside(start)
+
+    def halo_wait(source, turn):
+        def wait(a, b, place):
+            got = source.at[pl.ds(2 * place, 2)]
+            pltpu.make_async_copy(got, got, halo_recv.at[turn, place]).wait()
+
+        each_beside(wait)
 
     def near(brick, a, b, c):
         return near_ref[0, 0, brick, (a + 1) * 9 + (b + 1) * 3 + c + 1]
@@ -232,18 +276,31 @@
                 for half in range(2):
                     at = 8 + 2 * k + half
                     source[8 + brick, at : at + 1] = ends[row + x : row + x + 1, 128 * half : 128 * half + 128]
-        halo(source, turn, True)
+        halo_start(source, turn)
 
     def ends_of(source):
         rows = []
         for brick in range(2):
             low, high = near(brick, -1, 0, 0), near(brick, 1, 0, 0)
-            low = jnp.concatenate([source[low, 10:11, :], source[low, 11:12, :]], 1)
-            high = jnp.concatenate([source[high, 8:9, :], source[high, 9:10, :]], 1)
-            rows.append((low, high))
-        low = jnp.concatenate([jnp.broadcast_to(rows[brick][0], (16, 256)) for brick in range(2)], 0)
-        high = jnp.concatenate([jnp.broadcast_to(rows[brick][1], (16, 256)) for brick in range(2)], 0)
-        return low, high
+            rows.append(jnp.concatenate([source[low, 10:11, :], source[low, 11:12, :]], 1))
+            rows.append(jnp.concatenate([source[high, 8:9, :], source[high, 9:10, :]], 1))
+        return jnp.concatenate(rows + [jnp.zeros((4, 256), F32)], 0)
+
+    x_wide = lax.broadcasted_iota(jnp.int32, (16, 384), 0)
+
+    def at_ends(rows, sign):
+        return jnp.concatenate(
+            [
+                jnp.where(
+                    x_wide == 0, sign * rows[2 * k : 2 * k + 1], jnp.where(x_wide == 15, rows[2 * k + 1 : 2 * k + 2], 0.0)
+                )
+                for k in range(2)
+            ],
+            0,
+        )
+
+    def pack(values):
+        return exact_dot(values, pack_ref[...])
 
     def merged(source, brick, a, rows, corners):
         lane = lax.broadcasted_iota(jnp.int32, (rows.stop - rows.start, 128), 1) % 64
@@ -291,19 +348,17 @@
         + jnp.where(z_at == 15, 0.0, pltpu.roll(vectors[2], 255, 1))
         - jnp.where(z_at == 0, 0.0, pltpu.roll(vectors[2], 1, 1))
     )
-    halo(vector_src, 0, False)
-    low, high = ends_of(vector_src)
+    change = jnp.concatenate([change, pack(change)], 1)
+    halo_wait(vector_src, 0)
+    ends = ends_of(vector_src)
     faces = jnp.concatenate([faces_of(vector_src, brick, False) for brick in range(2)], 0)
     change = (
         change
-        + jnp.where(x_at == 15, high, 0.0)
-        - jnp.where(x_at == 0, low, 0.0)
+        + at_ends(jnp.concatenate([ends, pack(ends)], 1), -1.0)
         + exact_dot(faces, slope_ref[...])
     )
-    residual = -4.0 * change
-
-    def pack(values):
-        return exact_dot(values, pack_ref[...])
+    change = -4.0 * change
+    residual, packed = change[:, :256], change[:, 256:]
 
     def plane_sum(values):
         summed = values + 0.5 * (
@@ -322,9 +377,9 @@
             + jnp.where(x_at == 15, 0.0, pltpu.roll(values, 31, 0))
         )
         own = shifted_diagonal * values - 2.0 * plane_sum(inner)
-        halo(source, 1 + turn, False)
-        low, high = ends_of(source)
-        ends = plane_sum(jnp.where(x_at == 0, low, jnp.where(x_at == 15, high, 0.0)))
+        own = jnp.concatenate([own, pack(own)], 1)
+        halo_wait(source, 1 + turn)
+        ends = at_ends(exact_dot(ends_of(source), plane_ref[...]), 1.0)
         row_at = lax.broadcasted_iota(jnp.int32, (16, 128), 0)
         half_row = lax.broadcasted_iota(jnp.int32, (1, 128), 1) < 64
         faces = []
@@ -342,14 +397,14 @@
                     + jnp.where(row_at == 15, high, pltpu.roll(here, 15, 0))
                 )
             )
-        return own - ends - 2.0 * exact_dot(jnp.concatenate(faces, 0), weight_ref[...])
+        both = own - ends - 2.0 * exact_dot(jnp.concatenate(faces, 0), weight_ref[...])
+        return both[:, :256], both[:, 256:]
 
     def send_sums(turn, one, two):
         for row, values in enumerate((one, two)):
             summed = jnp.sum(values, axis=0, keepdims=True)
             part_out[turn, row : row + 1] = summed[:, :128] + summed[:, 128:]
         part_in[turn, pl.ds(me, 1)] = part_out[pl.ds(turn, 1)]
-
         each_device(
             lambda to: pltpu.make_async_remote_copy(
                 src_ref=part_out.at[turn],
@@ -367,14 +422,12 @@
         total = jnp.sum(jnp.sum(part_in[turn], axis=0), axis=1, keepdims=True)
         return total[0:1], total[1:2]
 
-    send_faces(1, residual, pack(residual))
-    image = operator(0, residual)
-
-    packed = pack(image)
+    send_faces(1, residual, packed)
+    image, packed = operator(0, residual)
+
     send_faces(2, image, packed)
     send_sums(0, residual * residual, residual * image)
-    second = operator(1, image)
-    packed_second = pack(second)
+    second, packed_second = operator(1, image)
     square_0, product = get_sums(0)
     step_0 = square_0 / product
     answer = step_0 * residual
@@ -385,7 +438,7 @@
 
     send_faces(3, image, packed)
     send_sums(1, residual * residual, residual * image)
-    second = operator(2, image)
+    second, _ = operator(2, image)
     square_1, product = get_sums(1)
     ratio = square_1 / square_0
     step_1 = square_1 / (product - ratio * square_1 / step_0)
@@ -416,14 +469,12 @@
     for turn in range(3):
         sent = part_in.at[turn, pl.ds(0, devices - 1)]
         pltpu.make_async_copy(sent, sent, part_send.at[turn]).wait()
-    for a, b in offsets:
-        place = (a + 1) * 3 + b + 1
-
-        @pl.when(inside(a, b))
-        def _(place=place):
-            for turn, source in enumerate(sources):
-                sent = source.at[pl.ds(8, 2)]
-                pltpu.make_async_copy(sent, sent, halo_send.at[turn, place]).wait()
+    def wait_sent(a, b, place):
+        for turn, source in enumerate(sources):
+            sent = source.at[pl.ds(8, 2)]
+            pltpu.make_async_copy(sent, sent, halo_send.at[turn, place]).wait()
+
+    each_beside(wait_sent)
 
 
 def shards(wides, narrows, point_owner, point_cell, normals, strip_count, neighbours):
@@ -444,8 +495,9 @@
             pltpu.VMEM((1, points), jnp.int32),
             pltpu.VMEM((3, points), F32),
             pltpu.VMEM((256, 128), BF16),
-            pltpu.VMEM((128, 256), BF16),
-            pltpu.VMEM((128, 256), BF16),
+            pltpu.VMEM((128, 384), BF16),
+            pltpu.VMEM((128, 384), BF16),
+            pltpu.VMEM((256, 384), BF16),
             pltpu.VMEM((wides, 4, slots), F32),
             pltpu.VMEM((wides, 4, slots), F32),
             pltpu.VMEM((19, 12, 128), F32),

time: 39.8 us -> 39.6 us (level)
  no operation moved by 1% of the time
where the time goes in v2:
time: 39.6 us; the launch traced here: 39.3 us
  Pallas kernels  34.7 us (88%)
  local copies, waits for them, and re-layouts  3.31 us (8%)
  between operations  1.32 us (3%)
    pallas_call x1, Pallas kernels, shards(): pl.pallas_call(functools.partial(kernel, wides, narrows), out_shape=(out,...  34.7 us
    unnamed x10, local copies, waits for them, and re-layouts  3.31 us

profile of v2, /device:TPU:0, one launch (start us, length us, event | category | flops | bytes accessed | tf_op | source)
XLA Modules:
  0.0 39.3 jit_solution(13353304133269285766)
XLA Ops:
  0.6 0.0 copy-start.1
  1.3 0.0 copy-start.3
  1.3 0.0 copy-done.1
  1.3 0.7 %copy-done.3 = s32[1,1,2,27]{3,2,1,0:T(2,128)S(1)} copy-done((s32[1,1,2,27]{3,2,1,0:T(2,128)S(1)}, s32[1,1,2,27]{3,2,1,0:T(2,128)}, u32[]{:S(2)}) %copy-start.3) | copy-done | bytes 240
  2.0 0.0 copy-start
  2.0 0.7 %copy-done = f32[3,1024]{1,0:T(4,128)S(1)} copy-done((f32[3,1024]{1,0:T(4,128)S(1)}, f32[3,1024]{1,0:T(4,128)}, u32[]{:S(2)}) %copy-start) | copy-done | bytes 12312
  2.7 0.0 copy-start.2
  2.7 0.7 %copy-done.2 = s32[1024]{0:T(1024)S(1)} copy-done((s32[1024]{0:T(1024)S(1)}, s32[1024]{0:T(1024)}, u32[]{:S(2)}) %copy-start.2) | copy-done | bytes 4120
  3.4 34.7 %shard_map.68 = (f32[1,1,2,4096]{3,2,1,0:T(2,128)S(1)}, f32[1,1,2,4096]{3,2,1,0:T(2,128)S(1)}) custom-call(s32[1,1024]{1,0:T(1,128)S(1)} %bitcast.2, s32[1,1024]{1,0:T(1,128)S(1)} %bitcast.3, f32[3,1024]{1,0:T(4,128)S(1)} %copy-done, s32[1]{0:T(128)S(6)} %copy.9.count_ref, s32[1,1,2,27]{3,2,1,0:T(2,128)S(1)} %copy-done.3), custom_call_target="tpu_custom_call" | custom-call | tf_op jit(solution)/shard_map/pallas_call | solution.py:488
  38.1 0.6 %copy.10 = f32[1,1,2,4096]{3,2,1,0:T(2,128)} copy(f32[1,1,2,4096]{3,2,1,0:T(2,128)S(1)} %get-tuple-element.4) | data formatting | bytes 65536
  38.7 0.6 %copy.11 = f32[1,1,2,4096]{3,2,1,0:T(2,128)} copy(f32[1,1,2,4096]{3,2,1,0:T(2,128)S(1)} %get-tuple-element.5) | data formatting | bytes 65536
Async XLA Ops:
  0.6 0.7 %copy-start.1 = (s32[1024,1]{0,1:T(1,128)S(1)}, s32[1024,1]{0,1:T(1,128)}, u32[]{:S(2)}) copy-start(s32[1024,1]{0,1:T(1,128)} %param.5) | copy-start | bytes 12292
  1.3 0.7 %copy-start.3 = (s32[1,1,2,27]{3,2,1,0:T(2,128)S(1)}, s32[1,1,2,27]{3,2,1,0:T(2,128)}, u32[]{:S(2)}) copy-start(s32[1,1,2,27]{3,2,1,0:T(2,128)} %near_ref.1) | copy-start | bytes 652
  2.0 0.7 %copy-start = (f32[3,1024]{1,0:T(4,128)S(1)}, f32[3,1024]{1,0:T(4,128)}, u32[]{:S(2)}) copy-start(f32[3,1024]{1,0:T(4,128)} %normal_hbm.1) | copy-start | bytes 36868
  2.7 0.7 %copy-start.2 = (s32[1024]{0:T(1024)S(1)}, s32[1024]{0:T(1024)}, u32[]{:S(2)}) copy-start(s32[1024]{0:T(1024)} %param.6) | copy-start | bytes 12292

commit v3 on v2

--- a/solution.py
+++ b/solution.py
@@ -515,7 +515,7 @@
             pltpu.SemaphoreType.DMA((3,)),
         ],
         compiler_params=pltpu.CompilerParams(
-            collective_id=0, has_side_effects=True, vmem_limit_bytes=32 * 1024 * 1024
+            collective_id=0, has_side_effects=True, vmem_limit_bytes=56 * 1024 * 1024
         ),
     )(
         point_owner.reshape(1, points), point_cell.reshape(1, points), normals, strip_count, neighbours

time: 39.6 us -> 39 us (0.985)
  local copies, waits for them, and re-layouts: 3.31 us -> 2 us
  Pallas kernels: 34.7 us -> 35.4 us
    unnamed x10 -> x4, local copies, waits for them, and re-layouts: 3.31 us -> 2 us
    pallas_call x1, Pallas kernels: 34.7 us -> 35.4 us  [shards(): pl.pallas_call(functools.partial(kernel, wides, narrows), out_shape=(out,...]
where the time goes in v3:
time: 39 us; the launch traced here: 38.7 us
  Pallas kernels  35.4 us (91%)
  local copies, waits for them, and re-layouts  2 us (5%)
  between operations  1.29 us (3%)
    pallas_call x1, Pallas kernels, shards(): pl.pallas_call(functools.partial(kernel, wides, narrows), out_shape=(out,...  35.4 us
    unnamed x4, local copies, waits for them, and re-layouts  2 us

profile of v3, /device:TPU:0, one launch (start us, length us, event | category | flops | bytes accessed | tf_op | source)
XLA Modules:
  0.0 38.7 jit_solution(1546015153764101269)
XLA Ops:
  1.3 35.4 %shard_map.68 = (f32[1,1,2,4096]{3,2,1,0:T(2,128)}, f32[1,1,2,4096]{3,2,1,0:T(2,128)}) custom-call(s32[1,1024]{1,0:T(1,128)} %bitcast.2, s32[1,1024]{1,0:T(1,128)} %bitcast.3, f32[3,1024]{1,0:T(4,128)} %normal_hbm.1, s32[1]{0:T(128)S(6)} %copy.9.count_ref, s32[1,1,2,27]{3,2,1,0:T(2,128)} %near_ref.1), custom_call_target="tpu_custom_call" | custom-call | tf_op jit(solution)/shard_map/pallas_call | solution.py:488
  36.7 0.0 copy-start
  36.7 1.4 %copy.10 = f32[1,1,2,4096]{3,2,1,0:T(2,128)} copy(f32[1,1,2,4096]{3,2,1,0:T(2,128)} %get-tuple-element.4) | data formatting | bytes 65536
  38.1 0.0 copy-done
  38.1 0.6 %copy.11 = f32[1,1,2,4096]{3,2,1,0:T(2,128)} copy(f32[1,1,2,4096]{3,2,1,0:T(2,128)S(1)} %copy-done) | data formatting | bytes 65536
Async XLA Ops:
  36.7 1.4 %copy-start = (f32[1,1,2,4096]{3,2,1,0:T(2,128)S(1)}, f32[1,1,2,4096]{3,2,1,0:T(2,128)}, u32[]{:S(2)}) copy-start(f32[1,1,2,4096]{3,2,1,0:T(2,128)} %get-tuple-element.5) | copy-start | bytes 98308

commit v4 on v3

--- a/solution.py
+++ b/solution.py
@@ -477,6 +477,17 @@
     each_beside(wait_sent)
 
 
+def hand_on(one_ref, two_ref, one_out, two_out, sems):
+    copies = [
+        pltpu.make_async_copy(one_ref, one_out, sems.at[0]),
+        pltpu.make_async_copy(two_ref, two_out, sems.at[1]),
+    ]
+    for copy in copies:
+        copy.start()
+    for copy in copies:
+        copy.wait()
+
+
 def shards(wides, narrows, point_owner, point_cell, normals, strip_count, neighbours):
     points = point_cell.shape[0]
     devices = wides * narrows
@@ -485,7 +496,7 @@
     hbm = pl.BlockSpec(memory_space=pltpu.HBM)
     smem = pl.BlockSpec(memory_space=pltpu.SMEM)
     out = jax.ShapeDtypeStruct((1, 1, 2, 4096), F32)
-    return pl.pallas_call(
+    results = pl.pallas_call(
         functools.partial(kernel, wides, narrows),
         out_shape=(out, out),
         in_specs=[hbm, hbm, hbm, smem, smem],
@@ -520,6 +531,14 @@
     )(
         point_owner.reshape(1, points), point_cell.reshape(1, points), normals, strip_count, neighbours
     )
+    return pl.pallas_call(
+        hand_on,
+        out_shape=(out, out),
+        in_specs=[hbm, hbm],
+        out_specs=(hbm, hbm),
+        scratch_shapes=[pltpu.SemaphoreType.DMA((2,))],
+        compiler_params=pltpu.CompilerParams(vmem_limit_bytes=56 * 1024 * 1024),
+    )(*results)
 
 
 def solution(mesh):

time: 39 us -> 40 us (1.026)
  Pallas kernels: 35.4 us -> 38.5 us
  local copies, waits for them, and re-layouts: 2 us -> 0 us
    pallas_call x0 -> x1, Pallas kernels: none -> 3.11 us  [shards(): pl.pallas_call(hand_on, out_shape=(out, out), in_specs=[hbm, hbm], out_sp...]
    unnamed x4 -> x0, local copies, waits for them, and re-layouts: 2 us -> none
where the time goes in v4:
time: 40 us; the launch traced here: 39.8 us
  Pallas kernels  38.5 us (96%)
  between operations  1.28 us (3%)
    pallas_call x1, Pallas kernels, shards(): pl.pallas_call(functools.partial(kernel, wides, narrows), out_shape=(out,...  35.4 us
    pallas_call x1, Pallas kernels, shards(): pl.pallas_call(hand_on, out_shape=(out, out), in_specs=[hbm, hbm], out_sp...  3.11 us

profile of v4, /device:TPU:0, one launch (start us, length us, event | category | flops | bytes accessed | tf_op | source)
XLA Modules:
  0.0 39.8 jit_solution(6434934551423592655)
XLA Ops:
  1.3 35.4 %shard_map.68 = (f32[1,1,2,4096]{3,2,1,0:T(2,128)}, f32[1,1,2,4096]{3,2,1,0:T(2,128)}) custom-call(s32[1,1024]{1,0:T(1,128)} %bitcast.2, s32[1,1024]{1,0:T(1,128)} %bitcast.3, f32[3,1024]{1,0:T(4,128)} %normal_hbm.1, s32[1]{0:T(128)S(6)} %copy.7.count_ref, s32[1,1,2,27]{3,2,1,0:T(2,128)} %near_ref.1), custom_call_target="tpu_custom_call" | custom-call | tf_op jit(solution)/shard_map/pallas_call | solution.py:499
  36.7 3.1 %shard_map.69 = (f32[1,1,2,4096]{3,2,1,0:T(2,128)}, f32[1,1,2,4096]{3,2,1,0:T(2,128)}) custom-call(f32[1,1,2,4096]{3,2,1,0:T(2,128)} %get-tuple-element.4.one_ref, f32[1,1,2,4096]{3,2,1,0:T(2,128)} %get-tuple-element.5.two_ref), custom_call_target="tpu_custom_call" | custom-call | tf_op jit(solution)/shard_map/pallas_call | solution.py:534
